TPU v7x, 512 devices: a whole 4x8x8 slice. The times are simulated.
512 devices in a mesh: node: 32 (over x, y), chan: 16 (over z, core).
Axes of the slice: x: 4, y: 8, z: 8, core: 2. Of those that a mesh axis runs over, the one named last changes fastest.
Arguments:
- features: bfloat16 [57344, 1024], P('node', 'chan'), may hold values from -0.046875 to 0.046875
- weight: bfloat16 [1024, 1024], P('node', 'chan'), may hold values from -0.375 to 0.375
- pre_clean: bfloat16 [57344, 1024], P('node', 'chan'), may hold values from -6 to 6
- pre_corrupt: bfloat16 [57344, 1024], P('node', 'chan'), may hold values from -6 to 6
- grad_clean: bfloat16 [57344, 1024], P('node', 'chan'), may hold values from -6 to 6
- grad_corrupt: bfloat16 [57344, 1024], P('node', 'chan'), may hold values from -6 to 6
- slopes: float32 [1024], P('chan'), may hold values from 0.05 to 0.5
- adj_vals: bfloat16 [448, 5, 128, 128], P('node'), may hold values from 0 to 0.07861328
- adj_cols: int32 [448, 5], P('node'), may hold values from 0 to 447, as said below
- adj_count: int32 [448], P('node'), may hold values from 1 to 5, as said below
- shuffle_from: int32 [448], replicated, may hold values from 0 to 447, as said below
Outputs:
- grad_weight: float32 [1024, 1024], P('node', 'chan')
- grad_features: bfloat16 [57344, 1024], P('node', 'chan')
Inputs may be any that keep to these rules, and one draw needn't show every extreme that they name: `adj_cols`: entry [b, k] is a block within 2 of b, and entry [b, 0] is b itself. Slots k < adj_count[b] of row block b hold edge tiles; the other slots are padding and are not read. `shuffle_from`: A permutation of the blocks. The 14 blocks of one index of node take their rows from exactly 14 distinct indices of node, 1 block from each; among these are the index just after it and the index 16 away, counted round.
All inputs are finite; a program needn't handle non-finite values.
Results may differ from a plain program's by a relative error of at most 0.023.
Values may be sent and summed in bfloat16 or wider, within the bound.
A program may use at most 64 MiB of HBM per device.

v0:
```python
import jax
import jax.numpy as jnp
from jax import lax
from jax.sharding import PartitionSpec as P


def shifted(value, axis, by):
    size = lax.axis_size(axis)
    pairs = [(i, i + by) for i in range(size) if 0 <= i + by < size]
    return lax.ppermute(value, axis, pairs)


def local_grad(grad_part, pre_part, slopes):
    factor = jnp.where(pre_part > 0, 1.0, slopes[None, :])
    return (grad_part.astype(jnp.float32) * factor).astype(jnp.bfloat16)


def local(
    features,
    weight,
    pre_clean,
    pre_corrupt,
    grad_clean,
    grad_corrupt,
    slopes,
    adj_vals,
    adj_cols,
    adj_count,
    shuffle_from,
):
    row_count, chan_width = features.shape
    blocks = adj_vals.shape[0]
    tile_slots = adj_vals.shape[1]
    tile_rows = adj_vals.shape[2]
    band_reach = (tile_slots - 1) // 2
    my_index = lax.axis_index("node")
    dev_count = lax.axis_size("node")
    d_clean = local_grad(grad_clean, pre_clean, slopes)
    d_corrupt = local_grad(grad_corrupt, pre_corrupt, slopes)
    stacked = jnp.concatenate([d_clean, d_corrupt], axis=1).reshape(
        blocks, tile_rows, 2 * chan_width
    )
    contrib = jnp.einsum("bkpq,bpc->bkqc", adj_vals, stacked, preferred_element_type=jnp.float32)
    span_blocks = blocks + 2 * band_reach
    targets = adj_cols - (my_index * blocks - band_reach)
    live_mask = jnp.arange(tile_slots)[None, :] < adj_count[:, None]
    chooser = (
        (targets.reshape(-1)[None, :] == jnp.arange(span_blocks)[:, None])
        & live_mask.reshape(-1)[None, :]
    ).astype(jnp.float32)
    summed = jnp.dot(
        chooser, contrib.reshape(blocks * tile_slots, -1), precision=lax.Precision.HIGHEST
    )
    summed = summed.reshape(span_blocks, tile_rows, 2 * chan_width)
    from_prev = shifted(summed[band_reach + blocks :].astype(jnp.bfloat16), "node", 1).astype(
        jnp.float32
    )
    from_next = shifted(summed[:band_reach].astype(jnp.bfloat16), "node", -1).astype(jnp.float32)
    remaining = blocks - band_reach
    middle = summed[band_reach : band_reach + blocks]
    middle = (
        middle
        + jnp.pad(from_prev, ((0, remaining), (0, 0), (0, 0)))
        + jnp.pad(from_next, ((remaining, 0), (0, 0), (0, 0)))
    )
    backprop = middle.astype(jnp.bfloat16).reshape(row_count, 2 * chan_width)
    back_clean = backprop[:, :chan_width]
    back_corrupt = backprop[:, chan_width:]
    my_blocks = my_index * blocks + jnp.arange(blocks)
    all_blocks = jnp.arange(shuffle_from.shape[0])
    one_hot = (shuffle_from[None, :] == my_blocks[:, None]).astype(jnp.int32)
    source_block = jnp.sum(one_hot * all_blocks[None, :], axis=1)
    wanted = (source_block[:, None] * tile_rows + jnp.arange(tile_rows)[None, :]).reshape(-1)
    portion = lax.all_gather(back_corrupt, "node", axis=0, tiled=True)
    inside = (wanted >= 0) & (wanted < portion.shape[0])
    fetched = jnp.take(portion, jnp.clip(wanted, 0, portion.shape[0] - 1), axis=0)
    unshuffled = jnp.where(inside[:, None], fetched, jnp.zeros_like(back_corrupt))
    combined = jnp.concatenate([back_clean, unshuffled], axis=1)
    product = lax.dot_general(
        lax.all_gather(features, "chan", axis=1, tiled=True),
        combined,
        (((0,), (0,)), ((), ())),
        preferred_element_type=jnp.float32,
    )
    partial_w = product[:, :chan_width] + product[:, chan_width:]
    share_rows = partial_w.shape[0] // dev_count
    summed_w = lax.psum(partial_w.astype(jnp.bfloat16), "node").astype(jnp.float32)
    grad_weight = lax.dynamic_slice_in_dim(summed_w, my_index * share_rows, share_rows, 0)
    portion = lax.all_gather(weight, "node", axis=0, tiled=True)
    doubled = jnp.concatenate([portion, portion], axis=1)
    partial_x = lax.dot_general(
        combined, doubled, (((1,), (1,)), ((), ())), preferred_element_type=jnp.float32
    )
    grad_features = lax.psum_scatter(
        partial_x.astype(jnp.bfloat16), "chan", scatter_dimension=1, tiled=True
    )
    return (grad_weight, grad_features)


def solution(mesh):
    placed = (
        P("node", "chan"),
        P("node", "chan"),
        P("node", "chan"),
        P("node", "chan"),
        P("node", "chan"),
        P("node", "chan"),
        P("chan"),
        P("node", None, None, None),
        P("node", None),
        P("node"),
        P(),
    )
    return jax.shard_map(
        local,
        mesh=mesh,
        in_specs=placed,
        out_specs=(P("node", "chan"), P("node", "chan")),
        check_vma=False,
    )
```

profile of v0, /device:TPU:2, one launch (start us, length us, event | category | flops | bytes accessed | tf_op | source)
XLA Modules:
  0.0 460.4 jit_solution(3532302501971480463)
XLA Ops:
  7.2 1.4 copy.28
  8.6 1.2 copy.29
  9.8 1.9 copy.30
  11.7 1.9 copy.31
  13.6 1.5 multiply_convert_fusion.1
  15.4 2.9 convolution_bitcast_fusion
  18.3 5.7 %copy.33 = f32[14,5,128,128]{3,2,1,0:T(8,128)} copy(f32[14,5,128,128]{2,3,1,0:T(8,128)} %convolution_bitcast_fusion) | data formatting | bytes 9175040 | tf_op jit(solution)/shard_map/bkpq,bpc->bkqc/dot_general | solution.py:43
  24.1 2.9 pad.25
  27.0 4.9 %copy.38 = f32[9,8,128,128]{3,1,2,0:T(8,128)} copy(f32[9,8,128,128]{3,2,1,0:T(8,128)S(1)} %bitcast.49) | data formatting | bytes 9437184
  32.3 4.1 fusion.24
  36.5 3.5 collective-permute-start
  40.0 4.5 collective-permute-start.1
  44.8 1.5 collective-permute-done.1
  46.4 1.0 fusion.23
  48.2 50.6 %all_gather.11 = bf16[1024,64]{1,0:T(8,128)(2,1)S(1)} all-gather(bf16[32,64]{1,0:T(8,128)(2,1)S(1)} %copy-done.1), channel_id=1, replica_groups=mesh['node'=32,'chan'=16] {'node'}, dimensions={0}, use_global_device_ids=true | all-gather | bytes 135168 | tf_op jit(solution)/shard_map/all_gather | solution.py:89
  99.3 86.6 %all-gather.3.cloned.1.call-done = bf16[57344,64]{1,0:T(8,128)(2,1)} async-done(((bf16[1792,64]{1,0:T(8,128)(2,1)}), bf16[57344,64]{1,0:T(8,128)(2,1)}) %all-gather.3.cloned.1.call-update) | async-done | bytes 7340048 | tf_op jit(solution)/shard_map/all_gather | solution.py:74
  185.9 11.3 %gather_fusion = bf16[1792,64]{1,0:T(8,128)(2,1)} fusion(bf16[57344,64]{1,0:T(8,128)(2,1)} %all-gather.3.cloned.1.call-done, s32[2048]{0:T(1024)S(1)} %pad_clamp_fusion), kind=kCustom, calls=%fused_computation | custom fusion | bytes 465920 | tf_op jit(solution)/shard_map/jit(_take)/gather | solution.py:76
  197.1 2.7 select_select_fusion
  199.8 32.0 %all-gather.5.cloned.1.call-done = bf16[1792,1024]{0,1:T(8,128)(2,1)} async-done(((bf16[1792,64]{0,1:T(8,128)(2,1)}), bf16[1792,1024]{0,1:T(8,128)(2,1)}) %all-gather.5.cloned.1.call-update) | async-done | bytes 3670032 | tf_op jit(solution)/shard_map/all_gather | solution.py:80
  231.8 3.7 convolution_bitcast_fusion.1
  236.2 3.0 convolution_convert_fusion
  239.3 147.1 %all-reduce.4.cloned.1.call-done = bf16[1024,64]{0,1:T(8,128)(2,1)} async-done(((bf16[1024,64]{0,1:T(8,128)(2,1)}), bf16[1024,64]{0,1:T(8,128)(2,1)}) %all-reduce.4.cloned.1.call-update) | async-done | bytes 131088 | tf_op jit(solution)/shard_map/psum | solution.py:87
  386.4 0.8 dynamic-slice_convert_fusion
  387.9 66.0 %reduce-scatter.2.cloned.1.call-done = bf16[1792,64]{0,1:T(8,128)(2,1)} async-done(((bf16[1792,1024]{0,1:T(8,128)(2,1)}), bf16[1792,64]{0,1:T(8,128)(2,1)}) %reduce-scatter.2.cloned.1.call-update) | async-done | bytes 229392 | tf_op jit(solution)/shard_map/reduce_scatter | solution.py:94
  (41 shorter events, 3.8 us)
Async XLA Ops:
  7.2 8.3 %copy-start = (bf16[14,5,128,128]{3,2,1,0:T(8,128)(2,1)S(1)}, bf16[14,5,128,128]{3,2,1,0:T(8,128)(2,1)}, u32[]{:S(2)}) copy-start(bf16[14,5,128,128]{3,2,1,0:T(8,128)(2,1)} %param.18) | copy-start | bytes 6881284
  7.2 178.7 %all-gather.3.cloned.1.call-start = ((), (), s32[]{:S(2)}) async-start(), calls=%async_computation.1 | async-start | bytes 15138816 | tf_op jit(solution)/shard_map/all_gather | solution.py:74
  27.0 4.9 %copy-start.2 = (s32[14,5]{0,1:T(8,128)S(1)}, s32[14,5]{0,1:T(8,128)}, u32[]{:S(2)}) copy-start(s32[14,5]{0,1:T(8,128)} %param.19) | copy-start | bytes 844
  27.0 5.1 %copy-start.4 = (s32[14]{0:T(128)S(1)}, s32[14]{0:T(128)}, u32[]{:S(2)}) copy-start(s32[14]{0:T(128)} %param.20) | copy-start | bytes 172
  36.5 8.3 %collective-permute-start = (bf16[2,128,128]{2,1,0:T(8,128)(2,1)S(1)}, bf16[2,128,128]{2,1,0:T(8,128)(2,1)S(1)}, u32[]{:S(2)}, u32[]{:S(2)}) collective-permute-start(bf16[2,128,128]{2,1,0:T(8,128)(2,1)S(1)} %bitcast.56), channel_id=1, source_target_pairs={{0,16},{16,32},{32,48},{48,64},{64,80},{80,96},{96,112},{112,128},... | collective-permute-start | bytes 196616 | tf_op jit(solution)/shard_map/ppermute | solution.py:10
  40.0 6.4 %collective-permute-start.1 = (bf16[2,128,128]{2,1,0:T(8,128)(2,1)S(1)}, bf16[2,128,128]{2,1,0:T(8,128)(2,1)S(1)}, u32[]{:S(2)}, u32[]{:S(2)}) collective-permute-start(bf16[2,128,128]{2,1,0:T(8,128)(2,1)S(1)} %bitcast.57), channel_id=1, source_target_pairs={{16,0},{32,16},{48,32},{64,48},{80,64},{96,80},{112,96},{128,112},... | collective-permute-start | bytes 196616 | tf_op jit(solution)/shard_map/ppermute | solution.py:10
  44.4 3.8 copy-start.1
  44.6 54.2 %copy-start.3 = (s32[448]{0:T(512)S(1)}, s32[448]{0:T(512)}, u32[]{:S(2)}) copy-start(s32[448]{0:T(512)} %param.21) | copy-start | bytes 5380
  47.4 184.4 %all-gather.5.cloned.1.call-start = ((), (), s32[]{:S(2)}) async-start(), calls=%async_computation.2 | async-start | bytes 3899392 | tf_op jit(solution)/shard_map/all_gather | solution.py:80
  48.2 338.2 %all-reduce.4.cloned.1.call-start = ((), (), s32[]{:S(2)}) async-start(), calls=%async_computation.3 | async-start | bytes 262144 | tf_op jit(solution)/shard_map/psum | solution.py:87
  236.2 217.7 %reduce-scatter.2.cloned.1.call-start = ((), (), s32[]{:S(2)}) async-start(), calls=%async_computation.4 | async-start | bytes 3899392 | tf_op jit(solution)/shard_map/reduce_scatter | solution.py:94
Sparse Core Ops, SparseCore 0:
  47.5 138.3 all-gather.2
  188.0 43.7 all-gather.4
  236.3 150.0 all-reduce.3
  389.9 63.8 reduce-scatter.1
where the time goes:
time: 461 us; the launch traced here: 460 us
  waiting for transfers between devices  334 us (72%)
  blocking collectives  50.6 us (11%)
  local copies, waits for them, and re-layouts  33.5 us (7%)
  between operations  14 us (3%)
  matrix products  13.7 us (3%)
  starting transfers between devices  8.11 us (2%)
  other arithmetic  6.56 us (1%)
    psum x1, waiting for transfers between devices, local(): lax.psum(partial_w.astype(jnp.bfloat16), 'node').astype(jnp.float32)  147 us
    all_gather x1, waiting for transfers between devices, local(): portion = lax.all_gather(back_corrupt, 'node', axis=0, tiled=True)  86.6 us
    reduce_scatter x1, waiting for transfers between devices, local(): lax.psum_scatter(partial_x.astype(jnp.bfloat16), 'chan', scatter_dimensio...  66 us
    all_gather x1, blocking collectives, local(): portion = lax.all_gather(weight, 'node', axis=0, tiled=True)  50.6 us
    all_gather x1, waiting for transfers between devices, local(): lax.all_gather(features, 'chan', axis=1, tiled=True)  32 us
    unnamed x21, local copies, waits for them, and re-layouts  15.2 us
    gather x1, local copies, waits for them, and re-layouts, local(): jnp.take(portion, jnp.clip(wanted, 0, portion.shape[0] - 1), axis=0)  11.3 us
  transfers between devices with their start and end apart: 6, of which 5 were waited for; matrix products, arithmetic and copies ran while one was open for 4% of the time, Pallas kernels for 0%

commit v1 on v0

--- a/solution.py
+++ b/solution.py
@@ -84,7 +84,9 @@
     )
     partial_w = product[:, :chan_width] + product[:, chan_width:]
     share_rows = partial_w.shape[0] // dev_count
-    summed_w = lax.psum(partial_w.astype(jnp.bfloat16), "node").astype(jnp.float32)
+    summed_w = jnp.sum(lax.all_gather(partial_w.astype(jnp.bfloat16), "node"), axis=0).astype(
+        jnp.float32
+    )
     grad_weight = lax.dynamic_slice_in_dim(summed_w, my_index * share_rows, share_rows, 0)
     portion = lax.all_gather(weight, "node", axis=0, tiled=True)
     doubled = jnp.concatenate([portion, portion], axis=1)

time: 461 us -> 395 us (0.86)
  waiting for transfers between devices: 334 us -> 264 us
  local copies, waits for them, and re-layouts: 33.5 us -> 38.2 us
    psum x1 -> x0, waiting for transfers between devices: 147 us -> none  [local(): lax.psum(partial_w.astype(jnp.bfloat16), 'node').astype(jnp.float32)]
    all_gather x1, waiting for transfers between devices: 86.6 us -> 137 us  [local(): portion = lax.all_gather(back_corrupt, 'node', axis=0, tiled=True)]
    all_gather x0 -> x1, waiting for transfers between devices: none -> 32.2 us  [local(): lax.all_gather(partial_w.astype(jnp.bfloat16), 'node')]
    reduce_scatter x1, waiting for transfers between devices: 66 us -> 60.4 us  [local(): lax.psum_scatter(partial_x.astype(jnp.bfloat16), 'chan', scatter_dimensio...]
    unnamed x21 -> x22, local copies, waits for them, and re-layouts: 15.2 us -> 19.9 us
  transfers between devices with their start and end apart: 6 -> 6, of which waited for: 5 -> 5; matrix products, arithmetic and copies ran while one was open for 4% -> 6% of each run, Pallas kernels for 0% -> 0%
where the time goes in v1:
time: 395 us; the launch traced here: 394 us
  waiting for transfers between devices  264 us (67%)
  blocking collectives  48.7 us (12%)
  local copies, waits for them, and re-layouts  38.2 us (10%)
  between operations  14 us (4%)
  matrix products  13.7 us (3%)
  starting transfers between devices  8.29 us (2%)
  other arithmetic  7.52 us (2%)
    all_gather x1, waiting for transfers between devices, local(): portion = lax.all_gather(back_corrupt, 'node', axis=0, tiled=True)  137 us
    reduce_scatter x1, waiting for transfers between devices, local(): lax.psum_scatter(partial_x.astype(jnp.bfloat16), 'chan', scatter_dimensio...  60.4 us
    all_gather x1, blocking collectives, local(): portion = lax.all_gather(weight, 'node', axis=0, tiled=True)  48.7 us
    all_gather x1, waiting for transfers between devices, local(): lax.all_gather(partial_w.astype(jnp.bfloat16), 'node')  32.2 us
    all_gather x1, waiting for transfers between devices, local(): lax.all_gather(features, 'chan', axis=1, tiled=True)  31.9 us
    unnamed x22, local copies, waits for them, and re-layouts  19.9 us
    gather x1, local copies, waits for them, and re-layouts, local(): jnp.take(portion, jnp.clip(wanted, 0, portion.shape[0] - 1), axis=0)  11.3 us
    ppermute x2, starting transfers between devices, shifted(): return lax.ppermute(value, axis, pairs)  7.95 us
  transfers between devices with their start and end apart: 6, of which 5 were waited for; matrix products, arithmetic and copies ran while one was open for 6% of the time, Pallas kernels for 0%

profile of v1, /device:TPU:2, one launch (start us, length us, event | category | flops | bytes accessed | tf_op | source)
XLA Modules:
  0.0 394.5 jit_solution(7482161486389567624)
XLA Ops:
  7.2 1.4 copy.34
  8.6 1.2 copy.35
  9.8 1.9 copy.36
  11.7 1.9 copy.37
  13.6 1.5 multiply_convert_fusion.1
  15.4 2.9 convolution_bitcast_fusion
  18.3 5.7 %copy.39 = f32[14,5,128,128]{3,2,1,0:T(8,128)} copy(f32[14,5,128,128]{2,3,1,0:T(8,128)} %convolution_bitcast_fusion) | data formatting | bytes 9175040 | tf_op jit(solution)/shard_map/bkpq,bpc->bkqc/dot_general | solution.py:43
  24.1 2.9 pad.25
  27.0 4.9 %copy.44 = f32[9,8,128,128]{3,1,2,0:T(8,128)} copy(f32[9,8,128,128]{3,2,1,0:T(8,128)S(1)} %bitcast.54) | data formatting | bytes 9437184
  32.3 4.1 %fusion.24 = (bf16[18,16384]{1,0:T(8,128)(2,1)S(1)}, f32[18,16384]{1,0:T(8,128)S(1)}) fusion(f32[70,16384]{1,0:T(8,128)} %bitcast.55, s32[70]{0:T(128)S(1)} %eq.28, pred[70]{0:T(512)(128)(4,1)S(1)} %lt.58), kind=kOutput, calls=%fused_computation.50 | convolution fusion | flops 248023520 | bytes 6357342 | tf_op jit(solution)/shard_map/dot_general | solution.py:51
  36.5 3.5 collective-permute-start
  40.0 4.5 %collective-permute-start.1 = (bf16[2,128,128]{2,1,0:T(8,128)(2,1)S(1)}, bf16[2,128,128]{2,1,0:T(8,128)(2,1)S(1)}, u32[]{:S(2)}, u32[]{:S(2)}) collective-permute-start(bf16[2,128,128]{2,1,0:T(8,128)(2,1)S(1)} %bitcast.63), channel_id=1, source_target_pairs={{16,0},{32,16},{48,32},{64,48},{80,64},{96,80},{112,96},{128,112},... | collective-permute-start | bytes 196616 | tf_op jit(solution)/shard_map/ppermute | solution.py:10
  44.8 1.6 collective-permute-done.1
  48.9 137.2 %all-gather.5.cloned.1.call-done = bf16[57344,64]{1,0:T(8,128)(2,1)} async-done(((bf16[1792,64]{1,0:T(8,128)(2,1)}), bf16[57344,64]{1,0:T(8,128)(2,1)}) %all-gather.5.cloned.1.call-update) | async-done | bytes 7340048 | tf_op jit(solution)/shard_map/all_gather | solution.py:74
  186.1 11.3 %gather_fusion = bf16[1792,64]{1,0:T(8,128)(2,1)} fusion(bf16[57344,64]{1,0:T(8,128)(2,1)} %all-gather.5.cloned.1.call-done, s32[2048]{0:T(1024)S(1)} %pad_clamp_fusion), kind=kCustom, calls=%fused_computation | custom fusion | bytes 465920 | tf_op jit(solution)/shard_map/jit(_take)/gather | solution.py:76
  197.4 2.7 select_select_fusion
  200.1 31.9 %all-gather.7.cloned.1.call-done = bf16[1792,1024]{0,1:T(8,128)(2,1)} async-done(((bf16[1792,64]{0,1:T(8,128)(2,1)}), bf16[1792,1024]{0,1:T(8,128)(2,1)}) %all-gather.7.cloned.1.call-update) | async-done | bytes 3670032 | tf_op jit(solution)/shard_map/all_gather | solution.py:80
  232.0 3.7 convolution_bitcast_fusion.1
  236.5 48.7 %all_gather.19 = bf16[1024,64]{1,0:T(8,128)(2,1)S(1)} all-gather(bf16[32,64]{1,0:T(8,128)(2,1)S(1)} %copy-done.1), channel_id=1, replica_groups=mesh['node'=32,'chan'=16] {'node'}, dimensions={0}, use_global_device_ids=true | all-gather | bytes 135168 | tf_op jit(solution)/shard_map/all_gather | solution.py:91
  285.2 3.0 convolution_convert_fusion
  288.2 32.2 %all-gather.9.cloned.1.call-done = bf16[32768,64]{0,1:T(8,128)(2,1)} async-done(((bf16[1024,64]{0,1:T(8,128)(2,1)}), bf16[32768,64]{0,1:T(8,128)(2,1)}) %all-gather.9.cloned.1.call-update) | async-done | bytes 4194320 | tf_op jit(solution)/shard_map/all_gather | solution.py:87
  320.5 4.6 %copy.49 = bf16[8,8,32,1024]{3,2,1,0:T(8,128)(2,1)S(1)} copy(bf16[8,8,32,1024]{3,1,2,0:T(8,128)(2,1)} %bitcast.57) | data formatting | bytes 8388608
  325.1 1.7 bitcast_reduce_fusion
  327.5 60.4 %reduce-scatter.2.cloned.1.call-done = bf16[1792,64]{0,1:T(8,128)(2,1)} async-done(((bf16[1792,1024]{0,1:T(8,128)(2,1)}), bf16[1792,64]{0,1:T(8,128)(2,1)}) %reduce-scatter.2.cloned.1.call-update) | async-done | bytes 229392 | tf_op jit(solution)/shard_map/reduce_scatter | solution.py:96
  (43 shorter events, 5.1 us)
Async XLA Ops:
  7.2 8.3 %copy-start = (bf16[14,5,128,128]{3,2,1,0:T(8,128)(2,1)S(1)}, bf16[14,5,128,128]{3,2,1,0:T(8,128)(2,1)}, u32[]{:S(2)}) copy-start(bf16[14,5,128,128]{3,2,1,0:T(8,128)(2,1)} %param.18) | copy-start | bytes 6881284
  7.2 179.0 %all-gather.5.cloned.1.call-start = ((), (), s32[]{:S(2)}) async-start(), calls=%async_computation.1 | async-start | bytes 15138816 | tf_op jit(solution)/shard_map/all_gather | solution.py:74
  27.0 4.9 %copy-start.2 = (s32[14,5]{0,1:T(8,128)S(1)}, s32[14,5]{0,1:T(8,128)}, u32[]{:S(2)}) copy-start(s32[14,5]{0,1:T(8,128)} %param.19) | copy-start | bytes 844
  27.0 5.1 %copy-start.4 = (s32[14]{0:T(128)S(1)}, s32[14]{0:T(128)}, u32[]{:S(2)}) copy-start(s32[14]{0:T(128)} %param.20) | copy-start | bytes 172
  36.5 12.0 %copy-start.3 = (s32[448]{0:T(512)S(1)}, s32[448]{0:T(512)}, u32[]{:S(2)}) copy-start(s32[448]{0:T(512)} %param.21) | copy-start | bytes 5380
  36.5 8.3 %collective-permute-start = (bf16[2,128,128]{2,1,0:T(8,128)(2,1)S(1)}, bf16[2,128,128]{2,1,0:T(8,128)(2,1)S(1)}, u32[]{:S(2)}, u32[]{:S(2)}) collective-permute-start(bf16[2,128,128]{2,1,0:T(8,128)(2,1)S(1)} %bitcast.62), channel_id=1, source_target_pairs={{0,16},{16,32},{32,48},{48,64},{64,80},{80,96},{96,112},{112,128},... | collective-permute-start | bytes 196616 | tf_op jit(solution)/shard_map/ppermute | solution.py:10
  40.0 6.4 %collective-permute-start.1 = (bf16[2,128,128]{2,1,0:T(8,128)(2,1)S(1)}, bf16[2,128,128]{2,1,0:T(8,128)(2,1)S(1)}, u32[]{:S(2)}, u32[]{:S(2)}) collective-permute-start(bf16[2,128,128]{2,1,0:T(8,128)(2,1)S(1)} %bitcast.63), channel_id=1, source_target_pairs={{16,0},{32,16},{48,32},{64,48},{80,64},{96,80},{112,96},{128,112},... | collective-permute-start | bytes 196616 | tf_op jit(solution)/shard_map/ppermute | solution.py:10
  47.4 184.6 %all-gather.7.cloned.1.call-start = ((), (), s32[]{:S(2)}) async-start(), calls=%async_computation.2 | async-start | bytes 3899392 | tf_op jit(solution)/shard_map/all_gather | solution.py:80
  48.2 272.3 %all-gather.9.cloned.1.call-start = ((), (), s32[]{:S(2)}) async-start(), calls=%async_computation.4 | async-start | bytes 4325376 | tf_op jit(solution)/shard_map/all_gather | solution.py:87
  197.4 39.1 %copy-start.1 = (bf16[32,64]{1,0:T(8,128)(2,1)S(1)}, bf16[32,64]{1,0:T(8,128)(2,1)}, u32[]{:S(2)}) copy-start(bf16[32,64]{1,0:T(8,128)(2,1)} %param.12) | copy-start | bytes 12292
  236.4 151.5 %reduce-scatter.2.cloned.1.call-start = ((), (), s32[]{:S(2)}) async-start(), calls=%async_computation.3 | async-start | bytes 3899392 | tf_op jit(solution)/shard_map/reduce_scatter | solution.py:96
Sparse Core Ops, SparseCore 0:
  47.5 138.5 all-gather.4
  188.3 43.7 all-gather.6
  236.5 83.8 all-gather.8
  323.7 64.1 reduce-scatter.1
